TPU v7x, 32 devices: a whole 2x2x4 slice. The times are simulated.
32 devices in a mesh: segment: 2 (over core), angle: 8 (over z, x), tile: 2 (over y).
Axes of the slice: x: 2, y: 2, z: 4, core: 2. Of those that a mesh axis runs over, the one named last changes fastest.
Arguments:
- sinogram: float32 [32, 32, 4096], P(('segment', 'angle'), 'tile'), may hold values from -6 to 6
- paganin_width: float32 [1], replicated, may hold values from 2 to 8
- window_block: int32 [32, 2], replicated, may hold values from 0 to 28
Outputs:
- volume: float32 [2, 32, 32768], P('tile', None, ('segment', 'angle'))
All inputs are finite; a program needn't handle non-finite values.
Results may differ from a plain program's by a relative error of at most 0.0035.
Values may be sent and summed in bfloat16 or wider, within the bound.
No kernel may reach another device: no remote copies, remote signals or barrier semaphores. Data moves between devices by JAX's collectives and lax.ppermute only.
A program may use at most 64 MiB of HBM per device.

v0:
```python
import math

import jax
import jax.numpy as jnp
from jax import lax
from jax.sharding import PartitionSpec as P

WIN = 512
BAND = 128
ROWS_DEV = 8
TCOLS = 256


def band_kernels(width):
    inner = jnp.arange(128, dtype=jnp.int32)
    offsets = (
        (jnp.arange(3, dtype=jnp.int32) - 1)[:, None, None] * 128
        + inner[None, :, None]
        - inner[None, None, :]
    )
    spread = offsets.astype(jnp.float32)
    inside = jnp.abs(offsets) <= BAND
    taps = jnp.arange(-BAND, BAND + 1).astype(jnp.float32)
    normal_total = jnp.sum(jnp.exp(-jnp.abs(taps) / width))
    paganin = jnp.where(inside, jnp.exp(-jnp.abs(spread) / width) / normal_total, 0.0)
    squared = jnp.maximum(spread * spread, 1.0)
    odd_taps = jnp.where(inside & (offsets % 2 == 1), -1.0 / (math.pi * math.pi * squared), 0.0)
    ramp = jnp.where(offsets == 0, 0.25, odd_taps)
    return (paganin, ramp)


def apply_band(rows, kernels):
    row_count, bins = rows.shape
    blocks = bins // 128
    shaped = rows.reshape(row_count, blocks, 128)
    padded = jnp.pad(shaped, ((0, 0), (1, 1), (0, 0)))
    result = jnp.zeros_like(shaped)
    for offset in range(3):
        result = result + jnp.einsum(
            "rbi,io->rbo",
            padded[:, offset : offset + blocks],
            kernels[offset],
            precision=lax.Precision.HIGHEST,
        )
    return result.reshape(row_count, bins)


def hat_block(angles, angle_total, row_first, row_count, tile_rows):
    theta = math.pi * angles.astype(jnp.float32) / angle_total
    rows_here = (row_first + jnp.arange(row_count, dtype=jnp.int32)).astype(jnp.float32) - (
        tile_rows - 1
    ) / 2.0
    columns = jnp.arange(TCOLS).astype(jnp.float32) - (TCOLS - 1) / 2.0
    across = (
        columns[None, None, :] * jnp.cos(theta)[:, None, None]
        + rows_here[None, :, None] * jnp.sin(theta)[:, None, None]
    )
    across = across.reshape(angles.shape[0], row_count * TCOLS) + WIN / 2.0
    detector = jnp.arange(WIN).astype(jnp.float32)
    weight = jnp.maximum(0.0, 1.0 - jnp.abs(across[:, None, :] - detector[None, :, None]))
    return weight.astype(jnp.bfloat16)


def accumulate(total, windows, first, row_first, angle_total, tile_rows):
    count = windows.shape[0]
    group = math.gcd(count, 4)
    turns = count // group
    blocks = windows.reshape(turns, group, windows.shape[1], WIN)

    def advance(carry, item):
        block, index = item
        angles = first + index * group + jnp.arange(group, dtype=jnp.int32)
        weights = hat_block(angles, angle_total, row_first, ROWS_DEV, tile_rows)
        return (
            carry + jnp.einsum("gsw,gwp->sp", block, weights, preferred_element_type=jnp.float32),
            None,
        )

    result, ignored = lax.scan(advance, total, (blocks, jnp.arange(turns, dtype=jnp.int32)))
    return result


def body(sinogram, paganin_width, window_block):
    angle_local, slice_local, bins = sinogram.shape
    group_size = lax.axis_size(("segment", "angle"))
    tile_count = lax.axis_size("tile")
    angle_total = angle_local * group_size
    tile_rows = ROWS_DEV * group_size
    position = lax.axis_index(("segment", "angle"))
    smoothing, ramping = band_kernels(paganin_width[0])
    rows = sinogram.reshape(angle_local * slice_local, bins)
    filtered = (
        apply_band(apply_band(rows, smoothing), ramping)
        .astype(jnp.bfloat16)
        .reshape(angle_local, slice_local, bins)
    )
    slice_total = slice_local * tile_count
    first_angle = position * angle_local
    starts = lax.dynamic_slice_in_dim(window_block, first_angle, angle_local, 0) * 128

    def cut_tiles(detector_row, window_starts):
        return jax.vmap(
            lambda window_start: lax.dynamic_slice_in_dim(detector_row, window_start, WIN, 1)
        )(window_starts)

    outgoing = jax.vmap(cut_tiles)(filtered, starts)
    arrived = lax.all_to_all(outgoing, "tile", split_axis=1, concat_axis=2, tiled=True)
    windows = arrived.reshape(angle_local, slice_total, WIN)
    segment_count = lax.axis_size("segment")
    angle_count = lax.axis_size("angle")
    segment_index = lax.axis_index("segment")
    angle_index = lax.axis_index("angle")
    half_first = segment_index * angle_count * angle_local
    pair_empty = jnp.zeros((segment_count, slice_total, ROWS_DEV * TCOLS), jnp.float32)
    piece = lax.all_gather(windows, "angle", axis=0, tiled=True)
    parts_done = []
    for other_segment in range(segment_count):
        other_first = (other_segment * angle_count + angle_index) * ROWS_DEV
        parts_done.append(
            accumulate(
                pair_empty[other_segment], piece, half_first, other_first, angle_total, tile_rows
            )
        )
    pair_terms = jnp.stack(parts_done)
    volume = lax.psum_scatter(pair_terms, "segment", scatter_dimension=0, tiled=True)[0]
    return volume[None]


def solution(mesh):
    in_specs = (P(("segment", "angle"), "tile", None), P(), P())
    out_specs = P("tile", None, ("segment", "angle"))
    return jax.shard_map(body, mesh=mesh, in_specs=in_specs, out_specs=out_specs, check_vma=False)
```

profile of v0, /device:TPU:0, one launch (start us, length us, event | category | flops | bytes accessed | tf_op | source)
XLA Modules:
  0.0 112.3 jit_solution(3302530166067085918)
XLA Ops:
  7.2 0.6 exponential_reduce_fusion
  7.9 1.1 %copy.16 = f32[4,8,32,128]{3,2,1,0:T(8,128)S(1)} copy(f32[4,8,32,128]{3,1,2,0:T(8,128)} %bitcast.96) | data formatting | bytes 1048576
  9.0 0.8 select_select_fusion
  11.0 0.6 fusion.21
  12.1 0.6 convolution_add_fusion.1
  12.7 0.6 fusion.22
  13.4 2.7 %copy.11 = bf16[2,16,4096]{1,0,2:T(2,128)(2,1)S(1)} copy(bf16[2,16,4096]{2,1,0:T(8,128)(2,1)S(1)} %convert_element_type.129) | data formatting | bytes 524288 | tf_op jit(solution)/shard_map/convert_element_type | solution.py:94
  16.5 1.6 %gather_fusion = bf16[4,16,512]{1,0,2:T(4,128)(2,1)S(1)} fusion(bf16[2,16,4096]{1,0,2:T(2,128)(2,1)S(1)} %copy.11, s32[4]{0:T(128)S(1)} %reshape.277), kind=kCustom, calls=%fused_computation | custom fusion | bytes 131120 | tf_op jit(solution)/shard_map/vmap(vmap())/gather | solution.py:103
  18.1 1.3 %copy.12 = bf16[2,2,16,512]{3,2,0,1:T(8,128)(2,1)} copy(bf16[2,2,16,512]{2,1,0,3:T(2,128)(2,1)S(1)} %bitcast.94) | data formatting | bytes 131072 | tf_op jit(solution)/shard_map/vmap(vmap())/gather | solution.py:103
  19.4 4.2 %all-to-all-start = ((bf16[2,2,16,512]{3,2,0,1:T(8,128)(2,1)}), bf16[2,2,16,512]{3,2,0,1:T(8,128)(2,1)S(1)}, u32[]{:S(2)}, u32[]{:S(2)}) async-start(bf16[2,2,16,512]{3,2,0,1:T(8,128)(2,1)} %copy.12), calls=%async_computation | async-start | bytes 131072 | tf_op jit(solution)/shard_map/all_to_all | solution.py:107
  23.6 4.1 %all-to-all-done = bf16[2,2,16,512]{3,2,0,1:T(8,128)(2,1)S(1)} async-done(((bf16[2,2,16,512]{3,2,0,1:T(8,128)(2,1)}), bf16[2,2,16,512]{3,2,0,1:T(8,128)(2,1)S(1)}, u32[]{:S(2)}, u32[]{:S(2)}) %all-to-all-start) | async-done | bytes 65568 | tf_op jit(solution)/shard_map/all_to_all | solution.py:107
  27.7 32.3 %all_gather.3 = bf16[16,32,512]{2,1,0:T(8,128)(2,1)S(1)} all-gather(bf16[2,32,512]{2,1,0:T(8,128)(2,1)S(1)} %bitcast.97), channel_id=1, replica_groups=mesh['segment'=2,'angle'=8,'tile'=2] {'angle'}, dimensions={0}, use_global_device_ids=true | all-gather | bytes 589824 | tf_op jit(solution)/shard_map/all_gather | solution.py:115
  60.0 18.3 %while.26 = (s32[]{:T(128)}, f32[32,2048]{1,0:T(8,128)S(1)}, bf16[4,4,32,512]{3,2,1,0:T(8,128)(2,1)S(1)}, s32[4]{0:T(128)S(1)}, s32[]{:T(128)}, /*index=5*/s32[]{:T(128)}, s32[]{:T(128)}, s32[1]{0:T(128)}, s32[]{:T(128)}) while((s32[]{:T(128)}, f32[32,2048]{1,0:T(8,128)S(1)}, bf16[4,4,32,512]{3,2,1,0:T(8,128)(2,1)S(1)}, ...), condition=%wide.region_2.3_spmd.clone, body=%wide.region_1.2_spmd.clone.sunk | while | flops 289556544 | bytes 801303 | solution.py:79
  60.0 0.6 dynamic_slice.48
  61.6 3.0 %fusion.49 = f32[32,2048]{1,0:T(8,128)S(1)} fusion(f32[512]{0:T(512)S(1)} %iota_convert_fusion.4, f32[4,2048]{1,0:T(4,128)S(1)} %bitcast.92, f32[32,2048]{1,0:T(8,128)S(1)} %get-tuple-element.356, bf16[4,4,32,512]{3,2,1,0:T(8,128)(2,1)S(1)} %get-tuple-element.366, s32[]{:T(128)} %get-tuple-element.355, pred[]{:T(512)S(6)} %compare.10), kind=kOutput, calls=%fused_computation.4.clone.1 | convolution fusion | flops 289538048 | bytes 690181 | tf_op jit(solution)/shard_map/while/body/eval_jaxpr/gsw,gwp->sp/dot_general | solution.py:75
  64.6 0.6 dynamic_slice.48
  66.2 3.0 %fusion.49 = f32[32,2048]{1,0:T(8,128)S(1)} fusion(f32[512]{0:T(512)S(1)} %iota_convert_fusion.4, f32[4,2048]{1,0:T(4,128)S(1)} %bitcast.92, f32[32,2048]{1,0:T(8,128)S(1)} %get-tuple-element.356, bf16[4,4,32,512]{3,2,1,0:T(8,128)(2,1)S(1)} %get-tuple-element.366, s32[]{:T(128)} %get-tuple-element.355, pred[]{:T(512)S(6)} %compare.10), kind=kOutput, calls=%fused_computation.4.clone.1 | convolution fusion | flops 289538048 | bytes 690181 | tf_op jit(solution)/shard_map/while/body/eval_jaxpr/gsw,gwp->sp/dot_general | solution.py:75
  69.2 0.6 dynamic_slice.48
  70.7 3.0 %fusion.49 = f32[32,2048]{1,0:T(8,128)S(1)} fusion(f32[512]{0:T(512)S(1)} %iota_convert_fusion.4, f32[4,2048]{1,0:T(4,128)S(1)} %bitcast.92, f32[32,2048]{1,0:T(8,128)S(1)} %get-tuple-element.356, bf16[4,4,32,512]{3,2,1,0:T(8,128)(2,1)S(1)} %get-tuple-element.366, s32[]{:T(128)} %get-tuple-element.355, pred[]{:T(512)S(6)} %compare.10), kind=kOutput, calls=%fused_computation.4.clone.1 | convolution fusion | flops 289538048 | bytes 690181 | tf_op jit(solution)/shard_map/while/body/eval_jaxpr/gsw,gwp->sp/dot_general | solution.py:75
  73.7 0.6 dynamic_slice.48
  75.3 3.0 %fusion.49 = f32[32,2048]{1,0:T(8,128)S(1)} fusion(f32[512]{0:T(512)S(1)} %iota_convert_fusion.4, f32[4,2048]{1,0:T(4,128)S(1)} %bitcast.92, f32[32,2048]{1,0:T(8,128)S(1)} %get-tuple-element.356, bf16[4,4,32,512]{3,2,1,0:T(8,128)(2,1)S(1)} %get-tuple-element.366, s32[]{:T(128)} %get-tuple-element.355, pred[]{:T(512)S(6)} %compare.10), kind=kOutput, calls=%fused_computation.4.clone.1 | convolution fusion | flops 289538048 | bytes 690181 | tf_op jit(solution)/shard_map/while/body/eval_jaxpr/gsw,gwp->sp/dot_general | solution.py:75
  78.3 18.3 %while.27 = (s32[]{:T(128)}, f32[32,2048]{1,0:T(8,128)S(1)}, bf16[4,4,32,512]{3,2,1,0:T(8,128)(2,1)S(1)}, s32[4]{0:T(128)S(1)}, s32[]{:T(128)}, /*index=5*/s32[]{:T(128)}, s32[]{:T(128)}, s32[1]{0:T(128)}, s32[]{:T(128)}) while((s32[]{:T(128)}, f32[32,2048]{1,0:T(8,128)S(1)}, bf16[4,4,32,512]{3,2,1,0:T(8,128)(2,1)S(1)}, ...), condition=%wide.region_4.5_spmd.clone, body=%wide.region_3.4_spmd.clone.sunk | while | flops 289556544 | bytes 801303 | solution.py:79
  78.3 0.6 dynamic_slice.50
  79.9 3.0 %fusion.52 = f32[32,2048]{1,0:T(8,128)S(1)} fusion(f32[512]{0:T(512)S(1)} %iota_convert_fusion.5, f32[4,2048]{1,0:T(4,128)S(1)} %bitcast.93, f32[32,2048]{1,0:T(8,128)S(1)} %get-tuple-element.329, bf16[4,4,32,512]{3,2,1,0:T(8,128)(2,1)S(1)} %get-tuple-element.339, s32[]{:T(128)} %get-tuple-element.328, pred[]{:T(512)S(6)} %compare.11), kind=kOutput, calls=%fused_computation.22.clone.1 | convolution fusion | flops 289538048 | bytes 690181 | tf_op jit(solution)/shard_map/while/body/eval_jaxpr/gsw,gwp->sp/dot_general | solution.py:75
  82.9 0.6 dynamic_slice.50
  84.5 3.0 %fusion.52 = f32[32,2048]{1,0:T(8,128)S(1)} fusion(f32[512]{0:T(512)S(1)} %iota_convert_fusion.5, f32[4,2048]{1,0:T(4,128)S(1)} %bitcast.93, f32[32,2048]{1,0:T(8,128)S(1)} %get-tuple-element.329, bf16[4,4,32,512]{3,2,1,0:T(8,128)(2,1)S(1)} %get-tuple-element.339, s32[]{:T(128)} %get-tuple-element.328, pred[]{:T(512)S(6)} %compare.11), kind=kOutput, calls=%fused_computation.22.clone.1 | convolution fusion | flops 289538048 | bytes 690181 | tf_op jit(solution)/shard_map/while/body/eval_jaxpr/gsw,gwp->sp/dot_general | solution.py:75
  87.5 0.6 dynamic_slice.50
  89.0 3.0 %fusion.52 = f32[32,2048]{1,0:T(8,128)S(1)} fusion(f32[512]{0:T(512)S(1)} %iota_convert_fusion.5, f32[4,2048]{1,0:T(4,128)S(1)} %bitcast.93, f32[32,2048]{1,0:T(8,128)S(1)} %get-tuple-element.329, bf16[4,4,32,512]{3,2,1,0:T(8,128)(2,1)S(1)} %get-tuple-element.339, s32[]{:T(128)} %get-tuple-element.328, pred[]{:T(512)S(6)} %compare.11), kind=kOutput, calls=%fused_computation.22.clone.1 | convolution fusion | flops 289538048 | bytes 690181 | tf_op jit(solution)/shard_map/while/body/eval_jaxpr/gsw,gwp->sp/dot_general | solution.py:75
  92.1 0.6 dynamic_slice.50
  93.6 3.0 %fusion.52 = f32[32,2048]{1,0:T(8,128)S(1)} fusion(f32[512]{0:T(512)S(1)} %iota_convert_fusion.5, f32[4,2048]{1,0:T(4,128)S(1)} %bitcast.93, f32[32,2048]{1,0:T(8,128)S(1)} %get-tuple-element.329, bf16[4,4,32,512]{3,2,1,0:T(8,128)(2,1)S(1)} %get-tuple-element.339, s32[]{:T(128)} %get-tuple-element.328, pred[]{:T(512)S(6)} %compare.11), kind=kOutput, calls=%fused_computation.22.clone.1 | convolution fusion | flops 289538048 | bytes 690181 | tf_op jit(solution)/shard_map/while/body/eval_jaxpr/gsw,gwp->sp/dot_general | solution.py:75
  96.6 0.8 pad_maximum_fusion
  97.5 8.0 %reduce-scatter.2.cloned.1.call-done = f32[1,32,2048]{2,1,0:T(8,128)} async-done(((f32[2,32,2048]{2,1,0:T(8,128)}), f32[1,32,2048]{2,1,0:T(8,128)}) %reduce-scatter.2.cloned.1.call-update) | async-done | bytes 262160 | tf_op jit(solution)/shard_map/reduce_scatter | solution.py:125
  (83 shorter events, 4.6 us)
Async XLA Ops:
  12.7 3.5 %copy-start = (s32[32,2]{0,1:T(2,128)S(1)}, s32[32,2]{0,1:T(2,128)}, u32[]{:S(2)}) copy-start(s32[32,2]{0,1:T(2,128)} %param.9) | copy-start | bytes 772
  19.4 8.4 %all-to-all-start = ((bf16[2,2,16,512]{3,2,0,1:T(8,128)(2,1)}), bf16[2,2,16,512]{3,2,0,1:T(8,128)(2,1)S(1)}, u32[]{:S(2)}, u32[]{:S(2)}) async-start(bf16[2,2,16,512]{3,2,0,1:T(8,128)(2,1)} %copy.12), calls=%async_computation | async-start | bytes 131072 | tf_op jit(solution)/shard_map/all_to_all | solution.py:107
  23.6 81.9 %reduce-scatter.2.cloned.1.call-start = ((), (), s32[]{:S(2)}) async-start(), calls=%async_computation.2 | async-start | bytes 786432 | tf_op jit(solution)/shard_map/reduce_scatter | solution.py:125
Sparse Core Ops, SparseCore 0:
  97.6 7.8 reduce-scatter.1
where the time goes:
time: 113 us; the launch traced here: 112 us
  blocking collectives  32.3 us (29%)
  matrix products  27.3 us (24%)
  between operations  14.2 us (13%)
  waiting for transfers between devices  12.1 us (11%)
  local copies, waits for them, and re-layouts  11.9 us (11%)
  loops' own time  5.61 us (5%)
  other arithmetic  4.68 us (4%)
  starting transfers between devices  4.24 us (4%)
    all_gather x1, blocking collectives, body(): piece = lax.all_gather(windows, 'angle', axis=0, tiled=True)  32.3 us
    dot_general x8, matrix products, advance(): jnp.einsum('gsw,gwp->sp', block, weights, preferred_element_type=jnp.floa...  23.9 us
    reduce_scatter x1, waiting for transfers between devices, body(): lax.psum_scatter(pair_terms, 'segment', scatter_dimension=0, tiled=True)[0]  7.99 us
    another operation x2, loops' own time, accumulate(): lax.scan(advance, total, (blocks, jnp.arange(turns, dtype=jnp.int32)))  5.61 us
    dynamic_slice x8, local copies, waits for them, and re-layouts, accumulate(): lax.scan(advance, total, (blocks, jnp.arange(turns, dtype=jnp.int32)))  4.69 us
    all_to_all x1, starting transfers between devices, body(): lax.all_to_all(outgoing, 'tile', split_axis=1, concat_axis=2, tiled=True)  4.23 us
    all_to_all x1, waiting for transfers between devices, body(): lax.all_to_all(outgoing, 'tile', split_axis=1, concat_axis=2, tiled=True)  4.12 us
    dot_general x6, matrix products, apply_band(): jnp.einsum('rbi,io->rbo', padded[:, offset:offset + blocks], kernels[offs...  3.39 us
  transfers between devices with their start and end apart: 2, of which 2 were waited for; matrix products, arithmetic and copies ran while one was open for 0% of the time, Pallas kernels for 0%

commit v1 on v0

v1 whole, which is shorter than its diff:
```python
import functools
import math

import jax
import jax.numpy as jnp
import numpy as np
from jax import lax
from jax.experimental import pallas as pl
from jax.experimental.pallas import tpu as pltpu
from jax.sharding import PartitionSpec as P

WIN = 512
BAND = 128
ROWS_DEV = 8
TCOLS = 256
LANES = 128
CHUNK = 64
DEPTH = 80


def split(value):
    high = value.astype(jnp.bfloat16)
    return high, (value - high.astype(jnp.float32)).astype(jnp.bfloat16)


def three_dots(rows, taps):
    (row_high, row_low), (tap_high, tap_low) = rows, taps
    dot = functools.partial(jnp.dot, preferred_element_type=jnp.float32)
    return dot(row_high, tap_high) + (dot(row_low, tap_high) + dot(row_high, tap_low))


def offsets(depth, width, shift):
    return (
        lax.broadcasted_iota(jnp.int32, (depth, width), 0)
        - lax.broadcasted_iota(jnp.int32, (depth, width), 1)
        - shift
    )


def filter_kernel(plan, place, blocks, width, rows_ref, *refs):
    tiles, outs, first_bin = plan
    outputs, (raw, smooth) = refs[:tiles], refs[tiles:]
    local, slices, bins = rows_ref.shape
    block_total = bins // LANES
    raw_blocks = raw.shape[1] // LANES
    smooth_blocks = smooth.shape[1] // LANES
    height = local * slices

    starts = []
    for turn in range(tiles):
        tile = lax.rem(place[1] - turn + tiles, tiles)
        for angle in range(local):
            start = blocks[place[0] + angle, tile]
            starts.append(start)
            at = turn * height + angle * slices
            for j in range(raw_blocks):
                block = start - 2 + j
                held = jnp.clip(block, 0, block_total - 1)
                lanes = pl.ds(pl.multiple_of(held * LANES, LANES), LANES)
                value = rows_ref[angle, :, lanes]
                inside = jnp.logical_and(block >= 0, block < block_total)
                raw[at : at + slices, j * LANES : (j + 1) * LANES] = jnp.where(inside, value, 0.0)

    decay = width[0]
    steps = (lax.broadcasted_iota(jnp.int32, (1, BAND), 1) + 1).astype(jnp.float32)
    total = 1.0 + 2.0 * jnp.sum(jnp.exp(-steps / decay), axis=1, keepdims=True)
    away = offsets(2 * 256, 256, BAND)
    spread = jnp.abs(away)
    paganin = jnp.where(
        spread <= BAND, jnp.exp(-spread.astype(jnp.float32) / decay) / total, 0.0
    )
    paganin = split(paganin)
    high, low = split(raw[...])
    for pair in range(smooth_blocks // 2):
        at = slice(pair * 256, pair * 256 + 512)
        smooth[:, pair * 256 : (pair + 1) * 256] = three_dots(
            (high[:, at], low[:, at]), paganin
        )
    for index, start in enumerate(starts):
        at = slice(index * slices, (index + 1) * slices)
        for j in range(smooth_blocks):
            if 1 <= j <= WIN // LANES:
                continue
            block = start - 1 + j
            inside = jnp.logical_and(block >= 0, block < block_total)
            lanes = slice(j * LANES, (j + 1) * LANES)
            smooth[at, lanes] = jnp.where(inside, smooth[at, lanes], 0.0)

    away = offsets(512, LANES, BAND + first_bin)
    spread = jnp.abs(away)
    squared = jnp.maximum(spread * spread, 1).astype(jnp.float32)
    odd = jnp.logical_and(spread <= BAND, (spread & 1) == 1)
    ramp = jnp.where(odd, -1.0 / (math.pi * math.pi * squared), 0.0)
    ramp = split(jnp.where(away == 0, 0.25, ramp))
    high, low = split(smooth[...])
    for j in range(outs):
        at = slice(j * LANES, j * LANES + 512)
        value = three_dots((high[:, at], low[:, at]), ramp)
        for turn in range(tiles):
            outputs[turn][:, j * LANES : (j + 1) * LANES] = value[
                turn * height : (turn + 1) * height
            ].astype(jnp.bfloat16)


def project_kernel(plan, place, table, *refs):
    segments, spots, tiles, local, slices, first_bin, tile_rows = plan
    groups = segments * spots
    pieces = refs[: groups * tiles]
    out, held = refs[groups * tiles], refs[groups * tiles + 1]
    angle_total = groups * local
    lane_blocks = held.shape[3] // LANES
    pixels = ROWS_DEV * CHUNK
    slice_total = slices * tiles

    for group in range(groups):
        for turn in range(tiles):
            piece = pieces[group * tiles + turn][...].astype(jnp.float32)
            for angle in range(local):
                held[group, angle, turn * slices : (turn + 1) * slices, :] = piece[
                    angle * slices : (angle + 1) * slices
                ]

    segment, spot, my_tile = place[0], place[1], place[2]
    first_row = ((segment * spots + spot) * ROWS_DEV).astype(jnp.float32) - (tile_rows - 1) / 2.0
    lane = lax.broadcasted_iota(jnp.int32, (8, pixels), 1)
    depth_step = lax.broadcasted_iota(jnp.int32, (8, pixels), 0).astype(jnp.float32)
    y = (lane // CHUNK).astype(jnp.float32) + first_row
    x_in_chunk = (lane % CHUNK).astype(jnp.float32)
    window_lane = lax.broadcasted_iota(jnp.int32, (slice_total, LANES), 1)
    gap = jnp.zeros((LANES - DEPTH, pixels), jnp.bfloat16)
    half = (WIN / 2.0) - first_bin

    sums = []
    for chunk in range(TCOLS // CHUNK):
        left = chunk * CHUNK - (TCOLS - 1) / 2.0
        right = left + CHUNK - 1
        x = x_in_chunk + left

        def step(group, total, x=x, left=left, right=right):
            from_segment = lax.rem(segment + group // spots, segments)
            from_spot = lax.rem(spot + lax.rem(group, spots), spots)
            source = (from_segment * spots + from_spot) * local
            windows, hats = [], []
            for angle in range(local):
                cosine = table[source + angle]
                sine = table[angle_total + source + angle]
                bottom = jnp.minimum(cosine * left, cosine * right) + jnp.minimum(
                    sine * first_row, sine * (first_row + (ROWS_DEV - 1))
                )
                low = (bottom + (half - 0.01)).astype(jnp.int32)
                block = low // LANES
                turn_by = (LANES - (low - block * LANES)) & (LANES - 1)
                near = pl.ds(pl.multiple_of(block * LANES, LANES), LANES)
                after = jnp.minimum(block + 1, lane_blocks - 1)
                far = pl.ds(pl.multiple_of(after * LANES, LANES), LANES)
                near = pltpu.roll(held[group, angle, :, near], turn_by, 1)
                far = pltpu.roll(held[group, angle, :, far], turn_by, 1)
                cut = jnp.where(turn_by == 0, LANES, turn_by)
                windows.append(jnp.where(window_lane < cut, near, far).astype(jnp.bfloat16))
                across = x * cosine + y * sine + (half - low.astype(jnp.float32)) - depth_step
                for j in range(DEPTH // 8):
                    hats.append(jnp.maximum(0.0, 1.0 - jnp.abs(across - 8.0 * j)))
                hats[-(DEPTH // 8) :] = [
                    jnp.concatenate(hats[-(DEPTH // 8) :], axis=0).astype(jnp.bfloat16),
                    gap,
                ]
            return total + jnp.dot(
                jnp.concatenate(windows, axis=1),
                jnp.concatenate(hats, axis=0),
                preferred_element_type=jnp.float32,
            )

        sums.append(lax.fori_loop(0, groups, step, jnp.zeros((slice_total, pixels), jnp.float32)))

    for pair in range(TCOLS // LANES):
        parts = sums[pair * (LANES // CHUNK) : (pair + 1) * (LANES // CHUNK)]
        for row in range(ROWS_DEV):
            value = jnp.concatenate(
                [part[:, row * CHUNK : (row + 1) * CHUNK] for part in parts], axis=1
            )
            at = row * TCOLS + pair * LANES
            if slices % 8 == 0:
                for turn in range(tiles):
                    tile = lax.rem(my_tile + turn, tiles)
                    into = pl.ds(pl.multiple_of(tile * slices, slices), slices)
                    out[0, into, at : at + LANES] = value[turn * slices : (turn + 1) * slices]
            else:
                out[0, :, at : at + LANES] = pltpu.roll(value, my_tile * slices, 0)


def shifted(value, axis, by):
    size = lax.axis_size(axis)
    return lax.ppermute(value, axis, [(i, (i - by) % size) for i in range(size)])


def body(sinogram, paganin_width, window_block):
    local, slices, bins = sinogram.shape
    segments, spots, tiles = (lax.axis_size(name) for name in ("segment", "angle", "tile"))
    segment, spot, tile = (lax.axis_index(name) for name in ("segment", "angle", "tile"))
    groups = segments * spots
    angle_total = local * groups
    tile_rows = ROWS_DEV * groups
    reach = math.hypot((TCOLS - 1) / 2, (tile_rows - 1) / 2)
    first_bin = max(0, int(WIN / 2 - reach - 0.01)) // 16 * 16
    last_bin = min(WIN - 1, int(WIN / 2 + reach + 0.01) + 1)
    outs = -(-(last_bin + 1 - first_bin) // LANES)
    assert first_bin + (outs - 1) * LANES < WIN and first_bin < LANES
    smooth_blocks = -(-(outs + 3) // 2) * 2

    smem = pl.BlockSpec(memory_space=pltpu.SMEM)
    vmem = pl.BlockSpec(memory_space=pltpu.VMEM)
    place = jnp.stack([(segment * spots + spot) * local, tile]).astype(jnp.int32)
    height = local * slices
    cut = pl.pallas_call(
        functools.partial(filter_kernel, (tiles, outs, first_bin)),
        out_shape=[jax.ShapeDtypeStruct((height, outs * LANES), jnp.bfloat16)] * tiles,
        in_specs=[smem, smem, smem, vmem],
        out_specs=[vmem] * tiles,
        scratch_shapes=[
            pltpu.VMEM((height * tiles, (smooth_blocks + 2) * LANES), jnp.float32),
            pltpu.VMEM((height * tiles, smooth_blocks * LANES), jnp.float32),
        ],
        compiler_params=pltpu.CompilerParams(vmem_limit_bytes=32 * 1024 * 1024),
        name="filter",
    )(place, window_block, paganin_width, sinogram)

    own = [cut[0]] + [shifted(cut[turn], "tile", turn) for turn in range(1, tiles)]
    own = jnp.stack(own)
    parts = [own] + [shifted(own, "angle", by) for by in range(1, spots)]
    everything = []
    for by in range(segments):
        everything += [part if by == 0 else shifted(part, "segment", by) for part in parts]
    pieces = [part[turn] for part in everything for turn in range(tiles)]

    theta = math.pi * np.arange(angle_total, dtype=np.float32) / np.float32(angle_total)
    table = np.concatenate([np.cos(theta), np.sin(theta)]).astype(np.float32)
    place = jnp.stack([segment, spot, tile]).astype(jnp.int32)
    plan = (segments, spots, tiles, local, slices, first_bin, tile_rows)
    return pl.pallas_call(
        functools.partial(project_kernel, plan),
        out_shape=jax.ShapeDtypeStruct((1, slices * tiles, ROWS_DEV * TCOLS), jnp.float32),
        in_specs=[smem, smem] + [vmem] * len(pieces),
        out_specs=vmem,
        scratch_shapes=[
            pltpu.VMEM((groups, local, slices * tiles, outs * LANES), jnp.float32),
        ],
        compiler_params=pltpu.CompilerParams(vmem_limit_bytes=32 * 1024 * 1024),
        name="project",
    )(place, jnp.asarray(table), *pieces)


def solution(mesh):
    in_specs = (P(("segment", "angle"), "tile", None), P(), P())
    out_specs = P("tile", None, ("segment", "angle"))
    return jax.shard_map(body, mesh=mesh, in_specs=in_specs, out_specs=out_specs, check_vma=False)
```

time: 113 us -> 43.3 us (0.38)
  blocking collectives: 32.3 us -> 0 us
  matrix products: 27.3 us -> 0 us
  Pallas kernels: 0 us -> 18.1 us
  between operations: 14.2 us -> 0.78 us
  starting transfers between devices: 4.24 us -> 17.4 us
  local copies, waits for them, and re-layouts: 11.9 us -> 1.88 us
  waiting for transfers between devices: 12.1 us -> 4.78 us
  loops' own time: 5.61 us -> 0 us
  other arithmetic: 4.68 us -> 0.16 us
    all_gather x1 -> x0, blocking collectives: 32.3 us -> none  [body(): piece = lax.all_gather(windows, 'angle', axis=0, tiled=True)]
    dot_general x14 -> x0, matrix products: 27.3 us -> none  [the longest x8 23.9 us: advance(): jnp.einsum('gsw,gwp->sp', block, weights, preferred_element_type=jnp.floa...]
    pallas_call x0 -> x2, Pallas kernels: none -> 18.1 us  [the longest x1 16.1 us: body(): pl.pallas_call(functools.partial(project_kernel, plan), out_shape=jax.Sha...]
    ppermute x0 -> x16, starting transfers between devices: none -> 17.4 us  [shifted(): lax.ppermute(value, axis, [(i, (i - by) % size) for i in range(size)])]
    reduce_scatter x1 -> x0, waiting for transfers between devices: 7.99 us -> none  [body(): lax.psum_scatter(pair_terms, 'segment', scatter_dimension=0, tiled=True)[0]]
    another operation x2 -> x0, loops' own time: 5.61 us -> none  [accumulate(): lax.scan(advance, total, (blocks, jnp.arange(turns, dtype=jnp.int32)))]
    ppermute x0 -> x16, waiting for transfers between devices: none -> 4.78 us  [shifted(): lax.ppermute(value, axis, [(i, (i - by) % size) for i in range(size)])]
    dynamic_slice x8 -> x0, local copies, waits for them, and re-layouts: 4.69 us -> none  [accumulate(): lax.scan(advance, total, (blocks, jnp.arange(turns, dtype=jnp.int32)))]
  transfers between devices with their start and end apart: 2 -> 16, of which waited for: 2 -> 7; matrix products, arithmetic and copies ran while one was open for 0% -> 0% of each run, Pallas kernels for 0% -> 0%
where the time goes in v1:
time: 43.3 us; the launch traced here: 43.1 us
  Pallas kernels  18.1 us (42%)
  starting transfers between devices  17.4 us (40%)
  waiting for transfers between devices  4.78 us (11%)
  local copies, waits for them, and re-layouts  1.88 us (4%)
  between operations  0.78 us (2%)
    ppermute x16, starting transfers between devices, shifted(): lax.ppermute(value, axis, [(i, (i - by) % size) for i in range(size)])  17.4 us
    pallas_call x1, Pallas kernels, body(): pl.pallas_call(functools.partial(project_kernel, plan), out_shape=jax.Sha...  16.1 us
    ppermute x16, waiting for transfers between devices, shifted(): lax.ppermute(value, axis, [(i, (i - by) % size) for i in range(size)])  4.78 us
    pallas_call x1, Pallas kernels, body(): pl.pallas_call(functools.partial(filter_kernel, (tiles, outs, first_bin))...  2 us
    unnamed x7, local copies, waits for them, and re-layouts  1.79 us
  transfers between devices with their start and end apart: 16, of which 7 were waited for; matrix products, arithmetic and copies ran while one was open for 0% of the time, Pallas kernels for 0%

profile of v1, /device:TPU:0, one launch (start us, length us, event | category | flops | bytes accessed | tf_op | source)
XLA Modules:
  0.0 43.1 jit_solution(10542417529561207809)
XLA Ops:
  0.7 0.0 copy-done.2
  0.7 0.1 copy.5.blocks
  0.8 0.1 pad_add_fusion.1.place
  0.8 1.0 %copy-done = f32[2,16,4096]{2,1,0:T(8,128)S(1)} copy-done((f32[2,16,4096]{2,1,0:T(8,128)S(1)}, f32[2,16,4096]{2,1,0:T(8,128)}, u32[]{:S(2)}) %copy-start) | copy-done | bytes 524312
  1.9 2.0 %filter.1 = (bf16[32,384]{1,0:T(8,128)(2,1)S(1)}, bf16[32,384]{1,0:T(8,128)(2,1)S(1)}) custom-call(s32[2]{0:T(128)S(1)} %pad_add_fusion.1.place, s32[32,2]{1,0:T(8,128)S(1)} %copy.5.blocks, f32[1]{0:T(128)S(6)} %copy.6.width, f32[2,16,4096]{2,1,0:T(8,128)S(1)} %copy-done), custom_call_target="tpu_custom_call" | custom-call | tf_op jit(solution)/shard_map/filter/pallas_call | solution.py:214
  3.9 3.0 %collective-permute-start = (bf16[32,384]{1,0:T(8,128)(2,1)S(1)}, bf16[32,384]{1,0:T(8,128)(2,1)S(1)}, u32[]{:S(2)}, u32[]{:S(2)}) collective-permute-start(bf16[32,384]{1,0:T(8,128)(2,1)S(1)} %get-tuple-element.8), channel_id=1, source_target_pairs={{0,1},{1,0},{2,3},{3,2},{4,5},{5,4},{6,7},{7,6},{8,9},{9,8},{10,11... | collective-permute-start | bytes 73736 | tf_op jit(solution)/shard_map/ppermute | solution.py:193
  6.9 1.8 %collective-permute-done.refs_1_ = bf16[32,384]{1,0:T(8,128)(2,1)S(1)} collective-permute-done((bf16[32,384]{1,0:T(8,128)(2,1)S(1)}, bf16[32,384]{1,0:T(8,128)(2,1)S(1)}, u32[]{:S(2)}, u32[]{:S(2)}) %collective-permute-start) | collective-permute-done | bytes 24608 | tf_op jit(solution)/shard_map/ppermute | solution.py:193
  8.7 0.1 collective-permute-start.8
  8.8 0.1 pad_add_fusion.place
  8.9 2.0 %collective-permute-start.7 = (bf16[2,32,384]{2,1,0:T(8,128)(2,1)S(1)}, bf16[2,32,384]{2,1,0:T(8,128)(2,1)S(1)}, u32[]{:S(2)}, u32[]{:S(2)}) collective-permute-start(bf16[2,32,384]{2,1,0:T(8,128)(2,1)S(1)} %pad_maximum_fusion), channel_id=1, source_target_pairs={{0,2},{2,4},{4,6},{6,8},{8,10},{10,12},{12,14},{14,0},{1,3},{3,5},... | collective-permute-start | bytes 147464 | tf_op jit(solution)/shard_map/ppermute | solution.py:193
  10.9 1.6 %collective-permute-start.6 = (bf16[2,32,384]{2,1,0:T(8,128)(2,1)S(1)}, bf16[2,32,384]{2,1,0:T(8,128)(2,1)S(1)}, u32[]{:S(2)}, u32[]{:S(2)}) collective-permute-start(bf16[2,32,384]{2,1,0:T(8,128)(2,1)S(1)} %pad_maximum_fusion), channel_id=1, source_target_pairs={{0,4},{2,6},{4,8},{6,10},{8,12},{10,14},{12,0},{14,2},{1,5},{3,7},... | collective-permute-start | bytes 147464 | tf_op jit(solution)/shard_map/ppermute | solution.py:193
  12.5 2.6 %collective-permute-start.5 = (bf16[2,32,384]{2,1,0:T(8,128)(2,1)S(1)}, bf16[2,32,384]{2,1,0:T(8,128)(2,1)S(1)}, u32[]{:S(2)}, u32[]{:S(2)}) collective-permute-start(bf16[2,32,384]{2,1,0:T(8,128)(2,1)S(1)} %pad_maximum_fusion), channel_id=1, source_target_pairs={{0,6},{2,8},{4,10},{6,12},{8,14},{10,0},{12,2},{14,4},{1,7},{3,9},... | collective-permute-start | bytes 147464 | tf_op jit(solution)/shard_map/ppermute | solution.py:193
  15.0 1.2 %collective-permute-start.4 = (bf16[2,32,384]{2,1,0:T(8,128)(2,1)S(1)}, bf16[2,32,384]{2,1,0:T(8,128)(2,1)S(1)}, u32[]{:S(2)}, u32[]{:S(2)}) collective-permute-start(bf16[2,32,384]{2,1,0:T(8,128)(2,1)S(1)} %pad_maximum_fusion), channel_id=1, source_target_pairs={{0,8},{2,10},{4,12},{6,14},{8,0},{10,2},{12,4},{14,6},{1,9},{3,11}... | collective-permute-start | bytes 147464 | tf_op jit(solution)/shard_map/ppermute | solution.py:193
  16.3 0.0 collective-permute-done.8
  16.3 2.6 %collective-permute-start.3 = (bf16[2,32,384]{2,1,0:T(8,128)(2,1)S(1)}, bf16[2,32,384]{2,1,0:T(8,128)(2,1)S(1)}, u32[]{:S(2)}, u32[]{:S(2)}) collective-permute-start(bf16[2,32,384]{2,1,0:T(8,128)(2,1)S(1)} %pad_maximum_fusion), channel_id=1, source_target_pairs={{0,10},{2,12},{4,14},{6,0},{8,2},{10,4},{12,6},{14,8},{1,11},{3,13... | collective-permute-start | bytes 147464 | tf_op jit(solution)/shard_map/ppermute | solution.py:193
  18.9 0.0 collective-permute-done.7
  18.9 1.4 %collective-permute-start.2 = (bf16[2,32,384]{2,1,0:T(8,128)(2,1)S(1)}, bf16[2,32,384]{2,1,0:T(8,128)(2,1)S(1)}, u32[]{:S(2)}, u32[]{:S(2)}) collective-permute-start(bf16[2,32,384]{2,1,0:T(8,128)(2,1)S(1)} %pad_maximum_fusion), channel_id=1, source_target_pairs={{0,12},{2,14},{4,0},{6,2},{8,4},{10,6},{12,8},{14,10},{1,13},{3,15... | collective-permute-start | bytes 147464 | tf_op jit(solution)/shard_map/ppermute | solution.py:193
  20.3 0.0 collective-permute-done.6
  20.3 1.5 %collective-permute-start.1 = (bf16[2,32,384]{2,1,0:T(8,128)(2,1)S(1)}, bf16[2,32,384]{2,1,0:T(8,128)(2,1)S(1)}, u32[]{:S(2)}, u32[]{:S(2)}) collective-permute-start(bf16[2,32,384]{2,1,0:T(8,128)(2,1)S(1)} %pad_maximum_fusion), channel_id=1, source_target_pairs={{0,14},{2,0},{4,2},{6,4},{8,6},{10,8},{12,10},{14,12},{1,15},{3,1}... | collective-permute-start | bytes 147464 | tf_op jit(solution)/shard_map/ppermute | solution.py:193
  21.8 0.1 collective-permute-start.15
  21.9 0.5 %collective-permute-start.14 = (bf16[2,32,384]{2,1,0:T(8,128)(2,1)S(1)}, bf16[2,32,384]{2,1,0:T(8,128)(2,1)S(1)}, u32[]{:S(2)}, u32[]{:S(2)}) collective-permute-start(bf16[2,32,384]{2,1,0:T(8,128)(2,1)S(1)} %collective-permute-done.6), channel_id=1, source_target_pairs={{0,16},{16,0},{1,17},{17,1},{2,18},{18,2},{3,19},{19,3},{4,20},{20... | collective-permute-start | bytes 147464 | tf_op jit(solution)/shard_map/ppermute | solution.py:193
  22.5 0.2 collective-permute-done.3
  22.6 1.4 %collective-permute-done.2 = bf16[2,32,384]{2,1,0:T(8,128)(2,1)S(1)} collective-permute-done((bf16[2,32,384]{2,1,0:T(8,128)(2,1)S(1)}, bf16[2,32,384]{2,1,0:T(8,128)(2,1)S(1)}, u32[]{:S(2)}, u32[]{:S(2)}) %collective-permute-start.2) | collective-permute-done | bytes 49184 | tf_op jit(solution)/shard_map/ppermute | solution.py:193
  24.1 0.4 collective-permute-done.1
  24.5 0.2 collective-permute-start.11
  24.6 0.4 collective-permute-start.10
  25.1 0.2 collective-permute-start.9
  25.3 0.3 collective-permute-done.11
  25.7 0.2 collective-permute-done.10
  25.9 0.4 collective-permute-done.9
  26.4 0.7 %copy-done.1 = f32[64]{0:T(128)S(1)} copy-done((f32[64]{0:T(128)S(1)}, f32[64]{0:T(128)}, u32[]{:S(2)}) %copy-start.1) | copy-done | bytes 280
  27.0 16.1 %project.1 = f32[1,32,2048]{2,1,0:T(8,128)} custom-call(s32[3]{0:T(128)S(1)} %pad_add_fusion.place, f32[64]{0:T(128)S(1)} %copy-done.1, bf16[32,384]{1,0:T(8,128)(2,1)S(1)} %get-tuple-element.7.refs_0_, bf16[32,384]{1,0:T(8,128)(2,1)S(1)} %collective-permute-done.refs_1_, bf16[32,384]{1,0:T(8,128)(2,1)S(1)} %get-tuple-element.38.refs_2_, ...), custom_call_target="tpu_custom_call" | custom-call | tf_op jit(solution)/shard_map/project/pallas_call | solution.py:239
  (27 shorter events, 0.1 us)
Async XLA Ops:
  0.0 0.7 %copy-start.2 = (s32[32,2]{0,1:T(2,128)S(1)}, s32[32,2]{0,1:T(2,128)}, u32[]{:S(2)}) copy-start(s32[32,2]{0,1:T(2,128)} %param.6) | copy-start | bytes 772
  0.8 1.0 %copy-start = (f32[2,16,4096]{2,1,0:T(8,128)S(1)}, f32[2,16,4096]{2,1,0:T(8,128)}, u32[]{:S(2)}) copy-start(f32[2,16,4096]{2,1,0:T(8,128)} %rows_ref.1) | copy-start | bytes 1572868
  3.9 4.8 %collective-permute-start = (bf16[32,384]{1,0:T(8,128)(2,1)S(1)}, bf16[32,384]{1,0:T(8,128)(2,1)S(1)}, u32[]{:S(2)}, u32[]{:S(2)}) collective-permute-start(bf16[32,384]{1,0:T(8,128)(2,1)S(1)} %get-tuple-element.8), channel_id=1, source_target_pairs={{0,1},{1,0},{2,3},{3,2},{4,5},{5,4},{6,7},{7,6},{8,9},{9,8},{10,11... | collective-permute-start | bytes 73736 | tf_op jit(solution)/shard_map/ppermute | solution.py:193
  8.7 7.5 %collective-permute-start.8 = (bf16[2,32,384]{2,1,0:T(8,128)(2,1)S(1)}, bf16[2,32,384]{2,1,0:T(8,128)(2,1)S(1)}, u32[]{:S(2)}, u32[]{:S(2)}) collective-permute-start(bf16[2,32,384]{2,1,0:T(8,128)(2,1)S(1)} %pad_maximum_fusion), channel_id=1, source_target_pairs={{0,16},{16,0},{1,17},{17,1},{2,18},{18,2},{3,19},{19,3},{4,20},{20... | collective-permute-start | bytes 147464 | tf_op jit(solution)/shard_map/ppermute | solution.py:193
  8.9 10.0 %collective-permute-start.7 = (bf16[2,32,384]{2,1,0:T(8,128)(2,1)S(1)}, bf16[2,32,384]{2,1,0:T(8,128)(2,1)S(1)}, u32[]{:S(2)}, u32[]{:S(2)}) collective-permute-start(bf16[2,32,384]{2,1,0:T(8,128)(2,1)S(1)} %pad_maximum_fusion), channel_id=1, source_target_pairs={{0,2},{2,4},{4,6},{6,8},{8,10},{10,12},{12,14},{14,0},{1,3},{3,5},... | collective-permute-start | bytes 147464 | tf_op jit(solution)/shard_map/ppermute | solution.py:193
  10.9 9.4 %collective-permute-start.6 = (bf16[2,32,384]{2,1,0:T(8,128)(2,1)S(1)}, bf16[2,32,384]{2,1,0:T(8,128)(2,1)S(1)}, u32[]{:S(2)}, u32[]{:S(2)}) collective-permute-start(bf16[2,32,384]{2,1,0:T(8,128)(2,1)S(1)} %pad_maximum_fusion), channel_id=1, source_target_pairs={{0,4},{2,6},{4,8},{6,10},{8,12},{10,14},{12,0},{14,2},{1,5},{3,7},... | collective-permute-start | bytes 147464 | tf_op jit(solution)/shard_map/ppermute | solution.py:193
  12.5 9.3 %collective-permute-start.5 = (bf16[2,32,384]{2,1,0:T(8,128)(2,1)S(1)}, bf16[2,32,384]{2,1,0:T(8,128)(2,1)S(1)}, u32[]{:S(2)}, u32[]{:S(2)}) collective-permute-start(bf16[2,32,384]{2,1,0:T(8,128)(2,1)S(1)} %pad_maximum_fusion), channel_id=1, source_target_pairs={{0,6},{2,8},{4,10},{6,12},{8,14},{10,0},{12,2},{14,4},{1,7},{3,9},... | collective-permute-start | bytes 147464 | tf_op jit(solution)/shard_map/ppermute | solution.py:193
  15.0 6.9 %collective-permute-start.4 = (bf16[2,32,384]{2,1,0:T(8,128)(2,1)S(1)}, bf16[2,32,384]{2,1,0:T(8,128)(2,1)S(1)}, u32[]{:S(2)}, u32[]{:S(2)}) collective-permute-start(bf16[2,32,384]{2,1,0:T(8,128)(2,1)S(1)} %pad_maximum_fusion), channel_id=1, source_target_pairs={{0,8},{2,10},{4,12},{6,14},{8,0},{10,2},{12,4},{14,6},{1,9},{3,11}... | collective-permute-start | bytes 147464 | tf_op jit(solution)/shard_map/ppermute | solution.py:193
  16.3 6.4 %collective-permute-start.3 = (bf16[2,32,384]{2,1,0:T(8,128)(2,1)S(1)}, bf16[2,32,384]{2,1,0:T(8,128)(2,1)S(1)}, u32[]{:S(2)}, u32[]{:S(2)}) collective-permute-start(bf16[2,32,384]{2,1,0:T(8,128)(2,1)S(1)} %pad_maximum_fusion), channel_id=1, source_target_pairs={{0,10},{2,12},{4,14},{6,0},{8,2},{10,4},{12,6},{14,8},{1,11},{3,13... | collective-permute-start | bytes 147464 | tf_op jit(solution)/shard_map/ppermute | solution.py:193
  18.9 5.1 %collective-permute-start.2 = (bf16[2,32,384]{2,1,0:T(8,128)(2,1)S(1)}, bf16[2,32,384]{2,1,0:T(8,128)(2,1)S(1)}, u32[]{:S(2)}, u32[]{:S(2)}) collective-permute-start(bf16[2,32,384]{2,1,0:T(8,128)(2,1)S(1)} %pad_maximum_fusion), channel_id=1, source_target_pairs={{0,12},{2,14},{4,0},{6,2},{8,4},{10,6},{12,8},{14,10},{1,13},{3,15... | collective-permute-start | bytes 147464 | tf_op jit(solution)/shard_map/ppermute | solution.py:193
  20.3 4.1 %collective-permute-start.1 = (bf16[2,32,384]{2,1,0:T(8,128)(2,1)S(1)}, bf16[2,32,384]{2,1,0:T(8,128)(2,1)S(1)}, u32[]{:S(2)}, u32[]{:S(2)}) collective-permute-start(bf16[2,32,384]{2,1,0:T(8,128)(2,1)S(1)} %pad_maximum_fusion), channel_id=1, source_target_pairs={{0,14},{2,0},{4,2},{6,4},{8,6},{10,8},{12,10},{14,12},{1,15},{3,1}... | collective-permute-start | bytes 147464 | tf_op jit(solution)/shard_map/ppermute | solution.py:193
  21.8 2.8 %collective-permute-start.15 = (bf16[2,32,384]{2,1,0:T(8,128)(2,1)S(1)}, bf16[2,32,384]{2,1,0:T(8,128)(2,1)S(1)}, u32[]{:S(2)}, u32[]{:S(2)}) collective-permute-start(bf16[2,32,384]{2,1,0:T(8,128)(2,1)S(1)} %collective-permute-done.7), channel_id=1, source_target_pairs={{0,16},{16,0},{1,17},{17,1},{2,18},{18,2},{3,19},{19,3},{4,20},{20... | collective-permute-start | bytes 147464 | tf_op jit(solution)/shard_map/ppermute | solution.py:193
  21.9 3.1 %collective-permute-start.14 = (bf16[2,32,384]{2,1,0:T(8,128)(2,1)S(1)}, bf16[2,32,384]{2,1,0:T(8,128)(2,1)S(1)}, u32[]{:S(2)}, u32[]{:S(2)}) collective-permute-start(bf16[2,32,384]{2,1,0:T(8,128)(2,1)S(1)} %collective-permute-done.6), channel_id=1, source_target_pairs={{0,16},{16,0},{1,17},{17,1},{2,18},{18,2},{3,19},{19,3},{4,20},{20... | collective-permute-start | bytes 147464 | tf_op jit(solution)/shard_map/ppermute | solution.py:193
  22.6 2.7 %collective-permute-start.13 = (bf16[2,32,384]{2,1,0:T(8,128)(2,1)S(1)}, bf16[2,32,384]{2,1,0:T(8,128)(2,1)S(1)}, u32[]{:S(2)}, u32[]{:S(2)}) collective-permute-start(bf16[2,32,384]{2,1,0:T(8,128)(2,1)S(1)} %collective-permute-done.5), channel_id=1, source_target_pairs={{0,16},{16,0},{1,17},{17,1},{2,18},{18,2},{3,19},{19,3},{4,20},{20... | collective-permute-start | bytes 147464 | tf_op jit(solution)/shard_map/ppermute | solution.py:193
  24.0 1.3 %collective-permute-start.12 = (bf16[2,32,384]{2,1,0:T(8,128)(2,1)S(1)}, bf16[2,32,384]{2,1,0:T(8,128)(2,1)S(1)}, u32[]{:S(2)}, u32[]{:S(2)}) collective-permute-start(bf16[2,32,384]{2,1,0:T(8,128)(2,1)S(1)} %collective-permute-done.4), channel_id=1, source_target_pairs={{0,16},{16,0},{1,17},{17,1},{2,18},{18,2},{3,19},{19,3},{4,20},{20... | collective-permute-start | bytes 147464 | tf_op jit(solution)/shard_map/ppermute | solution.py:193
  24.5 1.2 %collective-permute-start.11 = (bf16[2,32,384]{2,1,0:T(8,128)(2,1)S(1)}, bf16[2,32,384]{2,1,0:T(8,128)(2,1)S(1)}, u32[]{:S(2)}, u32[]{:S(2)}) collective-permute-start(bf16[2,32,384]{2,1,0:T(8,128)(2,1)S(1)} %collective-permute-done.3), channel_id=1, source_target_pairs={{0,16},{16,0},{1,17},{17,1},{2,18},{18,2},{3,19},{19,3},{4,20},{20... | collective-permute-start | bytes 147464 | tf_op jit(solution)/shard_map/ppermute | solution.py:193
  24.6 1.3 %collective-permute-start.10 = (bf16[2,32,384]{2,1,0:T(8,128)(2,1)S(1)}, bf16[2,32,384]{2,1,0:T(8,128)(2,1)S(1)}, u32[]{:S(2)}, u32[]{:S(2)}) collective-permute-start(bf16[2,32,384]{2,1,0:T(8,128)(2,1)S(1)} %collective-permute-done.2), channel_id=1, source_target_pairs={{0,16},{16,0},{1,17},{17,1},{2,18},{18,2},{3,19},{19,3},{4,20},{20... | collective-permute-start | bytes 147464 | tf_op jit(solution)/shard_map/ppermute | solution.py:193
  25.1 1.3 %collective-permute-start.9 = (bf16[2,32,384]{2,1,0:T(8,128)(2,1)S(1)}, bf16[2,32,384]{2,1,0:T(8,128)(2,1)S(1)}, u32[]{:S(2)}, u32[]{:S(2)}) collective-permute-start(bf16[2,32,384]{2,1,0:T(8,128)(2,1)S(1)} %collective-permute-done.1), channel_id=1, source_target_pairs={{0,16},{16,0},{1,17},{17,1},{2,18},{18,2},{3,19},{19,3},{4,20},{20... | collective-permute-start | bytes 147464 | tf_op jit(solution)/shard_map/ppermute | solution.py:193
  26.4 0.7 %copy-start.1 = (f32[64]{0:T(128)S(1)}, f32[64]{0:T(128)}, u32[]{:S(2)}) copy-start(f32[64]{0:T(128)} %constant.18.clone.table) | copy-start | bytes 772

commit v2 on v1

v2 whole, which is shorter than its diff:
```python
import functools
import math

import jax
import jax.numpy as jnp
import numpy as np
from jax import lax
from jax.experimental import pallas as pl
from jax.experimental.pallas import tpu as pltpu
from jax.sharding import PartitionSpec as P

WIN = 512
BAND = 128
ROWS_DEV = 8
TCOLS = 256
LANES = 128
CHUNK = 64
DEPTH = 80


def split(value):
    high = value.astype(jnp.bfloat16)
    return high, (value - high.astype(jnp.float32)).astype(jnp.bfloat16)


def three_dots(rows, taps):
    (row_high, row_low), (tap_high, tap_low) = rows, taps
    dot = functools.partial(jnp.dot, preferred_element_type=jnp.float32)
    return dot(row_high, tap_high) + (dot(row_low, tap_high) + dot(row_high, tap_low))


def offsets(depth, width, shift):
    return (
        lax.broadcasted_iota(jnp.int32, (depth, width), 0)
        - lax.broadcasted_iota(jnp.int32, (depth, width), 1)
        - shift
    )


def filter_kernel(plan, place, blocks, width, rows_ref, *refs):
    outs, first_bin = plan
    output, raw, smooth = refs
    spots, tiles = output.shape[:2]
    local, slices, bins = rows_ref.shape
    block_total = bins // LANES
    raw_blocks = raw.shape[1] // LANES
    smooth_blocks = smooth.shape[1] // LANES
    height = local * slices

    starts = []
    for turn in range(tiles):
        for angle in range(local):
            start = blocks[(place[0] * spots + place[1]) * local + angle, turn]
            starts.append(start)
            at = turn * height + angle * slices
            for j in range(raw_blocks):
                block = start - 2 + j
                held = jnp.clip(block, 0, block_total - 1)
                lanes = pl.ds(pl.multiple_of(held * LANES, LANES), LANES)
                value = rows_ref[angle, :, lanes]
                inside = jnp.logical_and(block >= 0, block < block_total)
                raw[at : at + slices, j * LANES : (j + 1) * LANES] = jnp.where(inside, value, 0.0)

    decay = width[0]
    steps = (lax.broadcasted_iota(jnp.int32, (1, BAND), 1) + 1).astype(jnp.float32)
    total = 1.0 + 2.0 * jnp.sum(jnp.exp(-steps / decay), axis=1, keepdims=True)
    away = offsets(2 * 256, 256, BAND)
    spread = jnp.abs(away)
    paganin = jnp.where(
        spread <= BAND, jnp.exp(-spread.astype(jnp.float32) / decay) / total, 0.0
    )
    paganin = split(paganin)
    high, low = split(raw[...])
    for pair in range(smooth_blocks // 2):
        at = slice(pair * 256, pair * 256 + 512)
        smooth[:, pair * 256 : (pair + 1) * 256] = three_dots(
            (high[:, at], low[:, at]), paganin
        )
    for index, start in enumerate(starts):
        at = slice(index * slices, (index + 1) * slices)
        for j in range(smooth_blocks):
            if 1 <= j <= WIN // LANES:
                continue
            block = start - 1 + j
            inside = jnp.logical_and(block >= 0, block < block_total)
            lanes = slice(j * LANES, (j + 1) * LANES)
            smooth[at, lanes] = jnp.where(inside, smooth[at, lanes], 0.0)

    away = offsets(512, LANES, BAND + first_bin)
    spread = jnp.abs(away)
    squared = jnp.maximum(spread * spread, 1).astype(jnp.float32)
    odd = jnp.logical_and(spread <= BAND, (spread & 1) == 1)
    ramp = jnp.where(odd, -1.0 / (math.pi * math.pi * squared), 0.0)
    ramp = split(jnp.where(away == 0, 0.25, ramp))
    high, low = split(smooth[...])
    for j in range(outs):
        at = slice(j * LANES, j * LANES + 512)
        value = three_dots((high[:, at], low[:, at]), ramp)
        for turn in range(tiles):
            part = value[turn * height : (turn + 1) * height].astype(jnp.bfloat16)
            for spot in range(spots):
                output[spot, turn, :, j * LANES : (j + 1) * LANES] = part


def geometry(place, sizes, angle_total):
    spots, first_bin, tile_rows = sizes
    first_row = ((place[0] * spots + place[1]) * ROWS_DEV).astype(jnp.float32) - (
        tile_rows - 1
    ) / 2.0
    half = (WIN / 2.0) - first_bin

    def lowest(cosine, sine, left):
        right = left + (CHUNK - 1)
        bottom = jnp.minimum(cosine * left, cosine * right) + jnp.minimum(
            sine * first_row, sine * (first_row + (ROWS_DEV - 1))
        )
        return (bottom + (half - 0.01)).astype(jnp.int32)

    return first_row, half, lowest


def chunk_left(chunk):
    return chunk * CHUNK - (TCOLS - 1) / 2.0


def angle_at(place, sizes, segments, part, index, local):
    segment = lax.rem(place[0] + part, segments)
    return segment * (sizes[0] * local) + index


def hat_kernel(plan, place, table, hats):
    sizes, local = plan
    segments, chunks, depth, pixels = hats.shape
    count = depth // LANES
    angle_total = segments * count
    first_row, half, lowest = geometry(place, sizes, angle_total)
    lane = lax.broadcasted_iota(jnp.int32, (8, pixels), 1)
    depth_step = lax.broadcasted_iota(jnp.int32, (8, pixels), 0).astype(jnp.float32)
    y = (lane // CHUNK).astype(jnp.float32) + first_row
    x = (lane % CHUNK).astype(jnp.float32)
    gap = jnp.zeros((LANES - DEPTH, pixels), jnp.bfloat16)
    for part in range(segments):

        def step(index, carry, part=part):
            angle = angle_at(place, sizes, segments, part, index, local)
            cosine, sine = table[angle], table[angle_total + angle]
            at = pl.multiple_of(index * LANES, LANES)
            for chunk in range(chunks):
                left = chunk_left(chunk)
                low = lowest(cosine, sine, left)
                across = (x + left) * cosine + y * sine + (half - low.astype(jnp.float32))
                across = across - depth_step
                rows = [
                    jnp.maximum(0.0, 1.0 - jnp.abs(across - 8.0 * j)) for j in range(DEPTH // 8)
                ]
                hats[part, chunk, pl.ds(at, DEPTH), :] = jnp.concatenate(rows, axis=0).astype(
                    jnp.bfloat16
                )
                hats[part, chunk, pl.ds(at + DEPTH, LANES - DEPTH), :] = gap
            return carry

        lax.fori_loop(0, count, step, 0)


def project_kernel(plan, place, table, windows, hats, *refs):
    sizes, local, part, last = plan
    before, (out, held, near_rows) = refs[:-3], refs[-3:]
    segments, chunks, depth, pixels = hats.shape
    spots, tiles = windows.shape[:2]
    slices = windows.shape[2] // local
    count = depth // LANES
    angle_total = segments * count
    lane_blocks = windows.shape[3] // LANES
    first_row, half, lowest = geometry(place, sizes, angle_total)
    for spot in range(spots):
        for turn in range(tiles):
            piece = windows[spot, turn].astype(jnp.float32)
            for angle in range(local):
                held[spot * local + angle, turn * slices : (turn + 1) * slices, :] = piece[
                    angle * slices : (angle + 1) * slices
                ]
    window_lane = lax.broadcasted_iota(jnp.int32, (slices * tiles, LANES), 1)

    def step(index, carry):
        angle = angle_at(place, sizes, segments, part, index, local)
        cosine, sine = table[angle], table[angle_total + angle]
        at = pl.ds(pl.multiple_of(index * LANES, LANES), LANES)
        for chunk in range(chunks):
            low = lowest(cosine, sine, chunk_left(chunk))
            block = low // LANES
            turn_by = (LANES - (low - block * LANES)) & (LANES - 1)
            near = pl.ds(pl.multiple_of(block * LANES, LANES), LANES)
            after = jnp.minimum(block + 1, lane_blocks - 1)
            far = pl.ds(pl.multiple_of(after * LANES, LANES), LANES)
            near = pltpu.roll(held[index, :, near], turn_by, 1)
            far = pltpu.roll(held[index, :, far], turn_by, 1)
            cut = jnp.where(turn_by == 0, LANES, turn_by)
            near_rows[chunk, :, at] = jnp.where(window_lane < cut, near, far).astype(jnp.bfloat16)
        return carry

    lax.fori_loop(0, count, step, 0, unroll=2)
    sums = []
    for chunk in range(chunks):
        value = jnp.dot(near_rows[chunk], hats[part, chunk], preferred_element_type=jnp.float32)
        if before:
            value = value + before[0][chunk]
        sums.append(value)
        if not last:
            out[chunk] = value
    if not last:
        return
    for pair in range(TCOLS // LANES):
        parts = sums[pair * (LANES // CHUNK) : (pair + 1) * (LANES // CHUNK)]
        for row in range(ROWS_DEV):
            at = row * TCOLS + pair * LANES
            out[0, :, at : at + LANES] = jnp.concatenate(
                [value[:, row * CHUNK : (row + 1) * CHUNK] for value in parts], axis=1
            )


def shifted(value, axis, by):
    size = lax.axis_size(axis)
    return lax.ppermute(value, axis, [(i, (i - by) % size) for i in range(size)])


def body(sinogram, paganin_width, window_block):
    local, slices, bins = sinogram.shape
    segments, spots, tiles = (lax.axis_size(name) for name in ("segment", "angle", "tile"))
    segment, spot = lax.axis_index("segment"), lax.axis_index("angle")
    groups = segments * spots
    angle_total = local * groups
    tile_rows = ROWS_DEV * groups
    reach = math.hypot((TCOLS - 1) / 2, (tile_rows - 1) / 2)
    first_bin = max(0, int(WIN / 2 - reach - 0.01)) // 16 * 16
    last_bin = min(WIN - 1, int(WIN / 2 + reach + 0.01) + 1)
    outs = -(-(last_bin + 1 - first_bin) // LANES)
    assert first_bin + (outs - 1) * LANES < WIN and first_bin < LANES
    smooth_blocks = -(-(outs + 3) // 2) * 2

    smem = pl.BlockSpec(memory_space=pltpu.SMEM)
    vmem = pl.BlockSpec(memory_space=pltpu.VMEM)
    hat_bytes = angle_total * LANES * ROWS_DEV * TCOLS * 2
    params = pltpu.CompilerParams(vmem_limit_bytes=hat_bytes + 12 * 1024 * 1024)
    place = jnp.stack([segment, spot]).astype(jnp.int32)
    height = local * slices
    cut = pl.pallas_call(
        functools.partial(filter_kernel, (outs, first_bin)),
        out_shape=jax.ShapeDtypeStruct((spots, tiles, height, outs * LANES), jnp.bfloat16),
        in_specs=[smem, smem, smem, vmem],
        out_specs=vmem,
        scratch_shapes=[
            pltpu.VMEM((height * tiles, (smooth_blocks + 2) * LANES), jnp.float32),
            pltpu.VMEM((height * tiles, smooth_blocks * LANES), jnp.float32),
        ],
        compiler_params=params,
        name="filter",
    )(place, window_block, paganin_width, sinogram)

    theta = math.pi * np.arange(angle_total, dtype=np.float32) / np.float32(angle_total)
    table = jnp.asarray(np.concatenate([np.cos(theta), np.sin(theta)]).astype(np.float32))
    sizes = (spots, first_bin, tile_rows)
    chunks, pixels = TCOLS // CHUNK, ROWS_DEV * CHUNK
    depth = spots * local * LANES
    hats = pl.pallas_call(
        functools.partial(hat_kernel, (sizes, local)),
        out_shape=jax.ShapeDtypeStruct((segments, chunks, depth, pixels), jnp.bfloat16),
        in_specs=[smem, smem],
        out_specs=vmem,
        compiler_params=params,
        cost_estimate=pl.CostEstimate(
            flops=segments * chunks * depth * pixels * 8, bytes_accessed=0, transcendentals=0
        ),
        name="hats",
    )(place, table)

    pieces = cut.reshape(spots * tiles, height, outs * LANES)
    pieces = lax.all_to_all(pieces, ("angle", "tile"), 0, 0, tiled=True)
    pieces = pieces.reshape(cut.shape)
    parts = [pieces] + [shifted(pieces, "segment", by) for by in range(1, segments)]
    sums = ()
    for part, windows in enumerate(parts):
        last = part == segments - 1
        sums = pl.pallas_call(
            functools.partial(project_kernel, (sizes, local, part, last)),
            out_shape=jax.ShapeDtypeStruct(
                (1, slices * tiles, ROWS_DEV * TCOLS)
                if last
                else (chunks, slices * tiles, pixels),
                jnp.float32,
            ),
            in_specs=[smem, smem] + [vmem] * (2 + len(sums)),
            out_specs=vmem,
            scratch_shapes=[
                pltpu.VMEM((spots * local, slices * tiles, outs * LANES), jnp.float32),
                pltpu.VMEM((chunks, slices * tiles, depth), jnp.bfloat16),
            ],
            compiler_params=params,
            cost_estimate=pl.CostEstimate(
                flops=16 * slices * tiles * chunks * depth * pixels,
                bytes_accessed=0,
                transcendentals=0,
            ),
            name="project",
        )(place, table, windows, hats, *sums)
        sums = (sums,)
    return sums[0]


def solution(mesh):
    in_specs = (P(("segment", "angle"), "tile", None), P(), P())
    out_specs = P("tile", None, ("segment", "angle"))
    return jax.shard_map(body, mesh=mesh, in_specs=in_specs, out_specs=out_specs, check_vma=False)
```

time: 43.3 us -> 39.2 us (0.905)
  blocking collectives: 0 us -> 20.7 us
  starting transfers between devices: 17.4 us -> 0.01 us
  waiting for transfers between devices: 4.78 us -> 0.01 us
  Pallas kernels: 18.1 us -> 14.9 us
  local copies, waits for them, and re-layouts: 1.88 us -> 2.46 us
    all_to_all x0 -> x1, blocking collectives: none -> 20.7 us  [body(): pieces = lax.all_to_all(pieces, ('angle', 'tile'), 0, 0, tiled=True)]
    ppermute x16 -> x1, starting transfers between devices: 17.4 us -> 0.01 us  [shifted(): lax.ppermute(value, axis, [(i, (i - by) % size) for i in range(size)])]
    ppermute x16 -> x1, waiting for transfers between devices: 4.78 us -> 0.01 us  [shifted(): lax.ppermute(value, axis, [(i, (i - by) % size) for i in range(size)])]
    pallas_call x2 -> x4, Pallas kernels: 18.1 us -> 14.9 us  [the longest x2 7.87 us: body(): pl.pallas_call(functools.partial(project_kernel, (sizes, local, part, las...]
    unnamed x7 -> x5, local copies, waits for them, and re-layouts: 1.79 us -> 2.46 us
  transfers between devices with their start and end apart: 16 -> 1, of which waited for: 7 -> 0; matrix products, arithmetic and copies ran while one was open for 0% -> 0% of each run, Pallas kernels for 0% -> 22%
where the time goes in v2:
time: 39.2 us; the launch traced here: 38.9 us
  blocking collectives  20.7 us (53%)
  Pallas kernels  14.9 us (38%)
  local copies, waits for them, and re-layouts  2.46 us (6%)
  between operations  0.68 us (2%)
    all_to_all x1, blocking collectives, body(): pieces = lax.all_to_all(pieces, ('angle', 'tile'), 0, 0, tiled=True)  20.7 us
    pallas_call x2, Pallas kernels, body(): pl.pallas_call(functools.partial(project_kernel, (sizes, local, part, las...  7.87 us
    pallas_call x1, Pallas kernels, body(): pl.pallas_call(functools.partial(hat_kernel, (sizes, local)), out_shape=j...  5.02 us
    unnamed x5, local copies, waits for them, and re-layouts  2.46 us
    pallas_call x1, Pallas kernels, body(): pl.pallas_call(functools.partial(filter_kernel, (outs, first_bin)), out_s...  2.01 us
  transfers between devices with their start and end apart: 1, of which 0 were waited for; matrix products, arithmetic and copies ran while one was open for 0% of the time, Pallas kernels for 22%

profile of v2, /device:TPU:0, one launch (start us, length us, event | category | flops | bytes accessed | tf_op | source)
XLA Modules:
  0.0 38.9 jit_solution(6318768773282909639)
XLA Ops:
  0.7 0.8 %copy.5.blocks = s32[32,2]{1,0:T(8,128)S(1)} copy(s32[32,2]{0,1:T(2,128)} %param.6) | data formatting | bytes 512 | tf_op args[2]
  1.4 0.1 pad_add_fusion.place
  1.5 0.0 copy-start
  1.5 1.0 %copy-done = f32[2,16,4096]{2,1,0:T(8,128)S(1)} copy-done((f32[2,16,4096]{2,1,0:T(8,128)S(1)}, f32[2,16,4096]{2,1,0:T(8,128)}, u32[]{:S(2)}) %copy-start) | copy-done | bytes 524312
  2.5 2.0 %filter.1 = bf16[8,2,32,384]{3,2,1,0:T(8,128)(2,1)S(1)} custom-call(s32[2]{0:T(128)S(1)} %pad_add_fusion.place, s32[32,2]{1,0:T(8,128)S(1)} %copy.5.blocks, f32[1]{0:T(128)S(6)} %copy.6.width, f32[2,16,4096]{2,1,0:T(8,128)S(1)} %copy-done), custom_call_target="tpu_custom_call" | custom-call | tf_op jit(solution)/shard_map/filter/pallas_call | solution.py:246
  4.5 20.7 %all_to_all.5 = bf16[16,32,384]{2,1,0:T(8,128)(2,1)S(1)} all-to-all(bf16[16,32,384]{2,1,0:T(8,128)(2,1)S(1)} %bitcast.4), channel_id=1, replica_groups=mesh['segment'=2,'angle'=8,'tile'=2] {'angle','tile'}, dimensions={0} | all-to-all | bytes 786432 | tf_op jit(solution)/shard_map/all_to_all | solution.py:277
  25.3 0.0 collective-permute-start
  25.3 0.0 copy-start.1
  25.3 0.7 %copy-done.1 = f32[64]{0:T(128)S(1)} copy-done((f32[64]{0:T(128)S(1)}, f32[64]{0:T(128)}, u32[]{:S(2)}) %copy-start.1) | copy-done | bytes 280
  25.9 5.0 %hats.1 = bf16[2,4,2048,512]{3,2,1,0:T(8,128)(2,1)S(1)} custom-call(s32[2]{0:T(128)S(1)} %pad_add_fusion.place, f32[64]{0:T(128)S(1)} %copy-done.1), custom_call_target="tpu_custom_call" | custom-call | flops 67108864 | tf_op jit(solution)/shard_map/hats/pallas_call | solution.py:264
  31.0 3.5 %project.2.refs_0_ = f32[4,32,512]{2,1,0:T(8,128)S(1)} custom-call(s32[2]{0:T(128)S(1)} %pad_add_fusion.place, f32[64]{0:T(128)S(1)} %copy-done.1, bf16[8,2,32,384]{3,2,1,0:T(8,128)(2,1)S(1)} %bitcast.6, bf16[2,4,2048,512]{3,2,1,0:T(8,128)(2,1)S(1)} %hats.1), custom_call_target="tpu_custom_call" | custom-call | flops 2147483648 | tf_op jit(solution)/shard_map/project/pallas_call | solution.py:283
  34.5 0.0 collective-permute-done.windows
  34.5 4.3 %project.3 = f32[1,32,2048]{2,1,0:T(8,128)} custom-call(s32[2]{0:T(128)S(1)} %pad_add_fusion.place, f32[64]{0:T(128)S(1)} %copy-done.1, bf16[8,2,32,384]{3,2,1,0:T(8,128)(2,1)S(1)} %collective-permute-done.windows, bf16[2,4,2048,512]{3,2,1,0:T(8,128)(2,1)S(1)} %hats.1, f32[4,32,512]{2,1,0:T(8,128)S(1)} %project.2.refs_0_), custom_call_target="tpu_custom_call" | custom-call | flops 2147483648 | tf_op jit(solution)/shard_map/project/pallas_call | solution.py:283
Async XLA Ops:
  1.5 1.0 %copy-start = (f32[2,16,4096]{2,1,0:T(8,128)S(1)}, f32[2,16,4096]{2,1,0:T(8,128)}, u32[]{:S(2)}) copy-start(f32[2,16,4096]{2,1,0:T(8,128)} %rows_ref.1) | copy-start | bytes 1572868
  25.3 9.2 %collective-permute-start = (bf16[8,2,32,384]{3,2,1,0:T(8,128)(2,1)S(1)}, bf16[8,2,32,384]{3,2,1,0:T(8,128)(2,1)S(1)}, u32[]{:S(2)}, u32[]{:S(2)}) collective-permute-start(bf16[8,2,32,384]{3,2,1,0:T(8,128)(2,1)S(1)} %bitcast.5), channel_id=1, source_target_pairs={{0,16},{16,0},{1,17},{17,1},{2,18},{18,2},{3,19},{19,3},{4,20},{20... | collective-permute-start | bytes 1179656 | tf_op jit(solution)/shard_map/ppermute | solution.py:223
  25.3 0.7 %copy-start.1 = (f32[64]{0:T(128)S(1)}, f32[64]{0:T(128)}, u32[]{:S(2)}) copy-start(f32[64]{0:T(128)} %constant.12.clone.table) | copy-start | bytes 772
